TPU v7x, 128 devices: a whole 4x4x4 slice. The times are simulated.
128 devices in a mesh: site: 2 (over core), sector: 64 (over z, x, y).
Axes of the slice: x: 4, y: 4, z: 4, core: 2. Of those that a mesh axis runs over, the one named last changes fastest.
Arguments:
- environment: bfloat16 [256, 128, 30, 128], P('sector'), may hold values from -6 to 6
- amplitudes: bfloat16 [2, 256, 4, 128, 128], P('site', 'sector'), may hold values from -0.5 to 0.5
- mpo_weight: bfloat16 [2, 30, 4, 4, 30], P('site'), may hold values from -0.75 to 0.75
- mpo_mask: int32 [2, 30, 30], P('site'), may hold values 0 or 1
- sector_count: int32 [64], replicated, may hold values from 1 to 4, as said below
Outputs:
- env_out: bfloat16 [2, 256, 128, 30, 128], P('site', 'sector')
Inputs may be any that keep to these rules, and one draw needn't show every extreme that they name: `sector_count`: every owner holds one or more sectors and some owner holds 4; owner 64 - 2 holds exactly one sector.
All inputs are finite; a program needn't handle non-finite values. No bound on the sum of `mpo_mask` on one device may be relied on, other than what follows from the above.
Results may differ from a plain program's by a relative error of at most 0.017.
Values may be sent and summed in bfloat16 or wider, within the bound.
No kernel may reach another device: no remote copies, remote signals or barrier semaphores. Data moves between devices by JAX's collectives and lax.ppermute only.
A program may use at most 128 MiB of HBM per device.

v0:
```python
import jax
import jax.numpy as jnp
from jax import lax
from jax.sharding import PartitionSpec as P


def passed_along(shard, axis, by):
    length = lax.axis_size(axis)
    pairs = [(i, i + by) for i in range(length) if 0 <= i + by < length]
    return lax.ppermute(shard, axis, pairs)


def mpo_effective(mpo_site, mask_site):
    charges = jnp.array([0, 1, 1, 2], jnp.int32)
    neutral = (charges[:, None] == charges[None, :]).astype(jnp.float32)
    keep_mask = mask_site.astype(jnp.float32)[:, None, None, :] * neutral[None, :, :, None]
    return (mpo_site.astype(jnp.float32) * keep_mask).astype(jnp.bfloat16)


def sector_partials(env_blocks, amp_blocks, amp_columns, mpo_eff):
    contracted = jnp.einsum(
        "kawc,ktcb->kawtb", env_blocks, amp_columns, preferred_element_type=jnp.float32
    ).astype(jnp.bfloat16)
    with_mpo = jnp.einsum(
        "kawtb,wstv->kasvb", contracted, mpo_eff, preferred_element_type=jnp.float32
    ).astype(jnp.bfloat16)

    def project(start_class, stop_class):
        return jnp.einsum(
            "ksab,kasvc->kbvc",
            amp_blocks[:, start_class:stop_class],
            with_mpo[:, :, start_class:stop_class],
            preferred_element_type=jnp.float32,
        ).astype(jnp.bfloat16)

    return (project(0, 1), project(1, 3), project(3, 4))


def pick_slot(blocks, slot_index):
    return lax.dynamic_index_in_dim(blocks, slot_index, 0, keepdims=False)


def advance(env_blocks, amp_blocks, amp_columns, mpo_eff, sector_count):
    owner_index = lax.axis_index("sector")
    slot_count = env_blocks.shape[0]
    zero_p, one_p, two_p = sector_partials(env_blocks, amp_blocks, amp_columns, mpo_eff)
    own_count = pick_slot(sector_count, owner_index)
    prior_count = pick_slot(sector_count, jnp.maximum(owner_index - 1, 0))
    got_one, got_two = passed_along((one_p, two_p), "sector", 1)
    far_blocks = passed_along(two_p, "sector", 2)
    far_count = pick_slot(sector_count, jnp.maximum(owner_index - 2, 0))
    in_one = pick_slot(got_one, prior_count - 1)
    in_two_near = pick_slot(got_two, prior_count - 1)
    in_two_back = pick_slot(got_two, jnp.maximum(prior_count - 2, 0))
    in_two_far = pick_slot(far_blocks, jnp.maximum(far_count - 1, 0))
    in_two_early = jnp.where(prior_count >= 2, in_two_back, in_two_far)
    one_in = jnp.concatenate([in_one[None], one_p[:-1]], 0)
    two_in = jnp.concatenate([in_two_early[None], in_two_near[None], two_p[:-2]], 0)
    summed = zero_p.astype(jnp.float32) + one_in.astype(jnp.float32) + two_in.astype(jnp.float32)
    live_slot = jnp.arange(slot_count, dtype=jnp.int32)[:, None, None, None] < own_count
    return jnp.where(live_slot, summed, 0.0).astype(jnp.bfloat16)


def shards(environment, amplitudes, mpo_weight, mpo_mask, sector_count):
    site_index = lax.axis_index("site")
    site_total = lax.axis_size("site")
    mpo_eff = mpo_effective(mpo_weight[0], mpo_mask[0])
    current = environment
    result = jnp.zeros(environment.shape, jnp.bfloat16)
    for section_index in range(site_total):
        updated = advance(current, amplitudes[0], amplitudes[0], mpo_eff, sector_count)
        result = jnp.where(site_index == section_index, updated, result)
        if section_index + 1 < site_total:
            current = passed_along(updated, "site", 1)
    return result[None]


def solution(mesh):
    placed = (
        P("sector", None, None, None),
        P("site", "sector", None, None, None),
        P("site", None, None, None, None),
        P("site", None, None),
        P(),
    )
    return jax.shard_map(
        shards,
        mesh=mesh,
        in_specs=placed,
        out_specs=P("site", "sector", None, None, None),
        check_vma=False,
    )
```

profile of v0, /device:TPU:70, one launch (start us, length us, event | category | flops | bytes accessed | tf_op | source)
XLA Modules:
  0.0 821.8 jit_solution(1336157564693496542)
XLA Ops:
  3.9 9.8 %fusion.28 = bf16[4,128,30,4,128]{4,1,3,2,0:T(8,128)(2,1)} fusion(bf16[4,128,30,128]{3,1,2,0:T(8,128)(2,1)} %param.6, bf16[4,4,128,128,1]{3,2,0,1,4:T(8,128)(2,1)S(1)} %bitcast.125), kind=kOutput, calls=%fused_computation.34 | convolution fusion | flops 2013265920 | bytes 20185088 | tf_op jit(solution)/shard_map/kawc,ktcb->kawtb/dot_general | solution.py:21
  13.7 22.2 %fusion.6 = bf16[4,128,4,30,128]{4,3,1,0,2:T(8,128)(2,1)} fusion(bf16[30,4,4,30,1,1]{0,3,2,5,4,1:T(8,128)(2,1)S(1)} %copy.30, bf16[4,128,30,4,128]{4,1,3,2,0:T(8,128)(2,1)} %fusion.28), kind=kOutput, calls=%fused_computation.8 | convolution fusion | flops 1895301120 | bytes 31486080 | tf_op jit(solution)/shard_map/kawtb,wstv->kasvb/dot_general | solution.py:24
  36.0 8.1 slice.57
  44.0 9.5 %fusion.22 = bf16[4,128,30,128]{1,3,2,0:T(8,128)(2,1)} fusion(bf16[4,128,2,30,128]{4,3,1,0,2:T(8,128)(2,1)} %slice.57, bf16[4,4,128,128]{3,2,0,1:T(8,128)(2,1)S(1)} %bitcast.126), kind=kOutput, calls=%fused_computation.28 | convolution fusion | flops 1008599040 | bytes 12058624 | tf_op jit(solution)/shard_map/ksab,kasvc->kbvc/dot_general | solution.py:29
  53.5 3.5 collective-permute-start
  57.0 5.5 slice_bitcast_fusion.3
  62.5 4.0 convert_bitcast_fusion.1
  66.5 4.9 collective-permute-start.2
  71.4 2.5 collective-permute-start.1
  74.0 3.9 slice.59
  84.0 145.8 %collective-permute-done = bf16[4,128,30,128]{1,3,2,0:T(8,128)(2,1)} collective-permute-done((bf16[4,128,30,128]{1,3,2,0:T(8,128)(2,1)}, bf16[4,128,30,128]{1,3,2,0:T(8,128)(2,1)}, u32[]{:S(2)}, u32[]{:S(2)}) %collective-permute-start) | collective-permute-done | bytes 3932192 | tf_op jit(solution)/shard_map/ppermute | solution.py:10
  231.2 166.1 %collective-permute-done.1 = bf16[4,128,30,128]{1,3,2,0:T(8,128)(2,1)} collective-permute-done((bf16[4,128,30,128]{1,3,2,0:T(8,128)(2,1)}, bf16[4,128,30,128]{1,3,2,0:T(8,128)(2,1)}, u32[]{:S(2)}, u32[]{:S(2)}) %collective-permute-start.1) | collective-permute-done | bytes 3932192 | tf_op jit(solution)/shard_map/ppermute | solution.py:10
  399.2 7.2 fusion.17
  410.0 6.0 collective-permute-done.3
  416.0 7.8 fusion.26
  423.8 21.8 %fusion.7 = bf16[4,128,4,30,128]{4,3,1,0,2:T(8,128)(2,1)} fusion(bf16[30,4,4,30,1,1]{0,3,2,5,4,1:T(8,128)(2,1)S(1)} %copy.30, bf16[4,128,30,4,128]{4,1,3,2,0:T(8,128)(2,1)} %fusion.26), kind=kOutput, calls=%fused_computation.9 | convolution fusion | flops 1895301120 | bytes 31486080 | tf_op jit(solution)/shard_map/kawtb,wstv->kasvb/dot_general | solution.py:24
  445.5 7.6 slice_bitcast_fusion.1
  454.3 6.5 fusion.25
  462.7 6.0 convert_bitcast_fusion
  472.6 2.2 slice.65
  476.7 160.4 %collective-permute-done.4 = bf16[4,128,30,128]{1,3,2,0:T(8,128)(2,1)} collective-permute-done((bf16[4,128,30,128]{1,3,2,0:T(8,128)(2,1)}, bf16[4,128,30,128]{1,3,2,0:T(8,128)(2,1)}, u32[]{:S(2)}, u32[]{:S(2)}) %collective-permute-start.4) | collective-permute-done | bytes 3932192 | tf_op jit(solution)/shard_map/ppermute | solution.py:10
  638.4 166.7 %collective-permute-done.5 = bf16[4,128,30,128]{1,3,2,0:T(8,128)(2,1)} collective-permute-done((bf16[4,128,30,128]{1,3,2,0:T(8,128)(2,1)}, bf16[4,128,30,128]{1,3,2,0:T(8,128)(2,1)}, u32[]{:S(2)}, u32[]{:S(2)}) %collective-permute-start.5) | collective-permute-done | bytes 3932192 | tf_op jit(solution)/shard_map/ppermute | solution.py:10
  807.1 8.2 fusion.24
  815.3 6.3 copy.18
  (32 shorter events, 25.9 us)
Async XLA Ops:
  53.5 176.4 %collective-permute-start = (bf16[4,128,30,128]{1,3,2,0:T(8,128)(2,1)}, bf16[4,128,30,128]{1,3,2,0:T(8,128)(2,1)}, u32[]{:S(2)}, u32[]{:S(2)}) collective-permute-start(bf16[4,128,30,128]{1,3,2,0:T(8,128)(2,1)} %fusion.22), channel_id=1, source_target_pairs={{0,1},{1,2},{2,3},{3,4},{4,5},{5,6},{6,7},{7,8},{8,9},{9,10},{10,1... | collective-permute-start | bytes 11796488 | tf_op jit(solution)/shard_map/ppermute | solution.py:10
  66.5 13.0 %copy-start.2 = (s32[64]{0:T(128)S(1)}, s32[64]{0:T(128)}, u32[]{:S(2)}) copy-start(s32[64]{0:T(128)} %param.10) | copy-start | bytes 772
  66.5 164.7 %collective-permute-start.2 = (bf16[4,128,30,128]{1,3,2,0:T(8,128)(2,1)}, bf16[4,128,30,128]{1,3,2,0:T(8,128)(2,1)}, u32[]{:S(2)}, u32[]{:S(2)}) collective-permute-start(bf16[4,128,30,128]{1,3,2,0:T(8,128)(2,1)} %convert_bitcast_fusion.1), channel_id=1, source_target_pairs={{0,2},{1,3},{2,4},{3,5},{4,6},{5,7},{6,8},{7,9},{8,10},{9,11},{10,... | collective-permute-start | bytes 11796488 | tf_op jit(solution)/shard_map/ppermute | solution.py:10
  71.4 325.8 %collective-permute-start.1 = (bf16[4,128,30,128]{1,3,2,0:T(8,128)(2,1)}, bf16[4,128,30,128]{1,3,2,0:T(8,128)(2,1)}, u32[]{:S(2)}, u32[]{:S(2)}) collective-permute-start(bf16[4,128,30,128]{1,3,2,0:T(8,128)(2,1)} %convert_bitcast_fusion.1), channel_id=1, source_target_pairs={{0,1},{1,2},{2,3},{3,4},{4,5},{5,6},{6,7},{7,8},{8,9},{9,10},{10,1... | collective-permute-start | bytes 11796488 | tf_op jit(solution)/shard_map/ppermute | solution.py:10
  83.3 316.0 %copy-start = (bf16[4,128,30,128]{3,2,1,0:T(8,128)(2,1)S(1)}, bf16[4,128,30,128]{3,2,1,0:T(8,128)(2,1)}, u32[]{:S(2)}) copy-start(bf16[4,128,30,128]{3,2,1,0:T(8,128)(2,1)} %get-tuple-element.7) | copy-start | bytes 11796484
  406.4 1.9 copy-start.3
  408.3 7.7 collective-permute-start.3
  445.5 8.8 %slice-start = ((bf16[4,128,4,30,128]{4,3,1,0,2:T(8,128)(2,1)}), bf16[4,128,2,30,128]{4,3,1,0,2:T(8,128)(2,1)S(1)}, s32[]{:S(2)}) async-start(bf16[4,128,4,30,128]{4,3,1,0,2:T(8,128)(2,1)} %fusion.7), calls=%async_computation | async-start | bytes 16777216 | tf_op jit(solution)/shard_map/slice | solution.py:32
  460.8 176.3 %collective-permute-start.4 = (bf16[4,128,30,128]{1,3,2,0:T(8,128)(2,1)}, bf16[4,128,30,128]{1,3,2,0:T(8,128)(2,1)}, u32[]{:S(2)}, u32[]{:S(2)}) collective-permute-start(bf16[4,128,30,128]{1,3,2,0:T(8,128)(2,1)} %fusion.25), channel_id=1, source_target_pairs={{0,1},{1,2},{2,3},{3,4},{4,5},{5,6},{6,7},{7,8},{8,9},{9,10},{10,1... | collective-permute-start | bytes 11796488 | tf_op jit(solution)/shard_map/ppermute | solution.py:10
  468.8 169.7 %collective-permute-start.6 = (bf16[4,128,30,128]{1,3,2,0:T(8,128)(2,1)}, bf16[4,128,30,128]{1,3,2,0:T(8,128)(2,1)}, u32[]{:S(2)}, u32[]{:S(2)}) collective-permute-start(bf16[4,128,30,128]{1,3,2,0:T(8,128)(2,1)} %convert_bitcast_fusion), channel_id=1, source_target_pairs={{0,2},{1,3},{2,4},{3,5},{4,6},{5,7},{6,8},{7,9},{8,10},{9,11},{10,... | collective-permute-start | bytes 11796488 | tf_op jit(solution)/shard_map/ppermute | solution.py:10
  470.7 334.4 %collective-permute-start.5 = (bf16[4,128,30,128]{1,3,2,0:T(8,128)(2,1)}, bf16[4,128,30,128]{1,3,2,0:T(8,128)(2,1)}, u32[]{:S(2)}, u32[]{:S(2)}) collective-permute-start(bf16[4,128,30,128]{1,3,2,0:T(8,128)(2,1)} %convert_bitcast_fusion), channel_id=1, source_target_pairs={{0,1},{1,2},{2,3},{3,4},{4,5},{5,6},{6,7},{7,8},{8,9},{9,10},{10,1... | collective-permute-start | bytes 11796488 | tf_op jit(solution)/shard_map/ppermute | solution.py:10
  474.8 332.3 %copy-start.4 = (bf16[4,128,30,128]{1,3,2,0:T(8,128)(2,1)S(1)}, bf16[4,128,30,128]{1,3,2,0:T(8,128)(2,1)}, u32[]{:S(2)}) copy-start(bf16[4,128,30,128]{1,3,2,0:T(8,128)(2,1)} %copy-done.3) | copy-start | bytes 11796484
  476.7 330.4 %copy-start.1 = (bf16[4,128,30,128]{3,2,1,0:T(8,128)(2,1)S(1)}, bf16[4,128,30,128]{3,2,1,0:T(8,128)(2,1)}, u32[]{:S(2)}) copy-start(bf16[4,128,30,128]{3,2,1,0:T(8,128)(2,1)} %get-tuple-element.5) | copy-start | bytes 11796484
where the time goes:
time: 829 us; the launch traced here: 822 us
  waiting for transfers between devices  645 us (78%)
  matrix products  103 us (12%)
  local copies, waits for them, and re-layouts  44.6 us (5%)
  starting transfers between devices  18.4 us (2%)
    ppermute x7, waiting for transfers between devices, passed_along(): return lax.ppermute(shard, axis, pairs)  645 us
    dot_general x2, matrix products, sector_partials(): jnp.einsum('kawtb,wstv->kasvb', contracted, mpo_eff, preferred_element_ty...  44 us
    dot_general x6, matrix products, project(): jnp.einsum('ksab,kasvc->kbvc', amp_blocks[:, start_class:stop_class], wit...  41.4 us
    ppermute x7, starting transfers between devices, passed_along(): return lax.ppermute(shard, axis, pairs)  18.4 us
    dot_general x2, matrix products, sector_partials(): jnp.einsum('kawc,ktcb->kawtb', env_blocks, amp_columns, preferred_element...  17.6 us
  transfers between devices with their start and end apart: 7, of which 5 were waited for; matrix products, arithmetic and copies ran while one was open for 4% of the time, Pallas kernels for 0%

commit v1 on v0

v1 whole, which is shorter than its diff:
```python
import functools

import jax
import jax.numpy as jnp
from jax import lax
from jax.experimental import pallas as pl
from jax.experimental.pallas import tpu as pltpu
from jax.sharding import PartitionSpec as P

S = 128
W = 30
HALF = 15
CUTS = ((0, 8), (8, HALF))
Q_FLOPS = 8_000_000_000
N_CUT = len(CUTS)
AXES = ("site", "sector")
F32 = jnp.float32
BF16 = jnp.bfloat16
MIB = 1024 * 1024
HBM = pl.BlockSpec(memory_space=pltpu.HBM)
VMEM = pl.BlockSpec(memory_space=pltpu.VMEM)
ANY = pl.BlockSpec(memory_space=pl.ANY)


def iota(shape, dim):
    return lax.broadcasted_iota(jnp.int32, shape, dim)


def place(sizes):
    owner = lax.axis_index("sector")
    return sizes[owner], lax.axis_index("site"), owner


def expand_operator(core, site, states, w_own, w_oth, wk):
    row_v = iota((8 * HALF, W), 0) // 8 + core * HALF
    pick_v = (row_v == iota((8 * HALF, W), 1)).astype(BF16)
    spot = iota((W, 8 * W), 1) // 8
    if site:
        spot = jnp.where(core == 0, spot, jnp.where(spot < HALF, spot + HALF, spot - HALF))
    pick_w = (spot == iota((W, 8 * W), 0)).astype(BF16)
    diagonal = (iota((8 * HALF, 8 * W), 0) % 8) == (iota((8 * HALF, 8 * W), 1) % 8)

    def block(s, s2):
        chosen = jnp.where(core == site, w_own[s, s2].astype(F32), w_oth[s, s2].astype(F32)).astype(BF16)
        rows = lax.dot_general(pick_v, chosen, (((1,), (1,)), ((), ())), preferred_element_type=F32).astype(BF16)
        full = jnp.dot(rows, pick_w, preferred_element_type=F32)
        return jnp.where(diagonal, full, 0.0).astype(BF16)

    if 0 in states:
        wk[0, : 8 * HALF, : 8 * W] = block(0, 0)
    if 3 in states:
        wk[1, : 8 * HALF, : 8 * W] = block(3, 3)
    if 1 in states:
        upper = jnp.concatenate([block(1, 1), block(1, 2)], axis=1)
        lower = jnp.concatenate([block(2, 1), block(2, 2)], axis=1)
        wk[2] = jnp.concatenate([upper, lower], axis=0)


def first_steps(left, amps, states, wk, z):
    columns = jnp.concatenate([amps[s] for s in states], axis=1) if len(states) > 1 else amps[states[0]]
    rights = []
    for g in range(8):
        block = left[:, 16 * g : 16 * g + 16, :].reshape(W * 16, S)
        c = jnp.dot(block, columns, preferred_element_type=F32)
        c = c.reshape(W, 16, S * len(states))
        low = c[:, :8, :].reshape(W * 8, S * len(states)).astype(BF16)
        high = c[:, 8:, :].reshape(W * 8, S * len(states)).astype(BF16)
        rights.append(
            {
                s: jnp.concatenate([low[:, S * k : S * k + S], high[:, S * k : S * k + S]], axis=1)
                for k, s in enumerate(states)
            }
        )

    def keep(s, g, total):
        total = total.reshape(HALF, 8, 2 * S)
        z[s, :, 16 * g : 16 * g + 16, :] = jnp.concatenate([total[:, :, :S], total[:, :, S:]], axis=1).astype(BF16)

    for g in range(8):
        for s, p in ((0, 0), (3, 1)):
            if s in states:
                keep(s, g, jnp.dot(wk[p, : 8 * HALF, : 8 * W], rights[g][s], preferred_element_type=F32))
        if 1 in states:
            both = jnp.concatenate([rights[g][1], rights[g][2]], axis=0)
            total = jnp.dot(wk[2], both, preferred_element_type=F32)
            keep(1, g, total[: 8 * HALF])
            keep(2, g, total[8 * HALF :])


def last_step(amps, states, z, sink):
    turned = [amps[s].astype(F32).T.astype(BF16) for s in states]
    lhs = jnp.concatenate(turned, axis=1) if len(states) > 1 else turned[0]

    def right(v):
        return jnp.concatenate([z[s, v] for s in states], axis=0) if len(states) > 1 else z[states[0], v]

    for v in range(0, HALF, 2):
        count = min(2, HALF - v)
        rhs = jnp.concatenate([right(v), right(v + 1)], axis=1) if count > 1 else right(v)
        out = jnp.dot(lhs, rhs, preferred_element_type=F32)
        for i in range(count):
            sink(v + i, out[:, S * i : S * i + S])


def form_left(slot, left, refs):
    @pl.when(slot == 0)
    def _():
        for half in range(2):
            for (a, b), ref in zip(CUTS, refs[0][half]):
                left[half * HALF + a : half * HALF + b] = ref[...]

    for k in (1, 2, 3):
        @pl.when(slot == k)
        def _(k=k):
            for half in range(2):
                left[half * HALF : half * HALF + HALF] = refs[k][half][...]


def grouped(refs):
    rest = refs[2 * N_CUT :]
    return ((refs[:N_CUT], refs[N_CUT : 2 * N_CUT]), *((rest[k], rest[3 + k]) for k in range(3)))


def pick_amp(core, site, amp_refs, slot, s):
    if site:
        return amp_refs[0][slot, s]
    return jnp.where(core == site, amp_refs[0][slot, s].astype(F32), amp_refs[1][slot, s].astype(F32)).astype(BF16)


def y_kernel(site, sizes, lefts, amp_refs, w_own, w_oth, outs, left, wk, z):
    count, core, _ = place(sizes)
    slot = count - 1
    expand_operator(core, site, (3,), w_own, w_oth, wk)
    amps = {3: pick_amp(core, site, amp_refs, slot, 3)}
    if site:
        form_left(slot, left, grouped(lefts))
    first_steps(left if site else lefts[0], amps, (3,), wk, z)

    def sink(v, block):
        for (a, b), out in zip(CUTS, outs):
            if a <= v < b:
                out[v - a] = block.astype(BF16)

    last_step(amps, (3,), z, sink)


def x_kernel(site, sizes, lefts, amp_refs, w_own, w_oth, outs, left, wk, z, acc, *sems):
    count, core, _ = place(sizes)
    prior = jnp.maximum(count - 2, 0)
    if site == 0:
        fetch = pltpu.make_async_copy(lefts[1].at[prior], left, sems[0])
        fetch.start()
    expand_operator(core, site, (1, 2, 3), w_own, w_oth, wk)
    if site:
        form_left(count - 1, left, grouped(lefts))
    amps = {s: pick_amp(core, site, amp_refs, count - 1, s) for s in (1, 2)}
    first_steps(left if site else lefts[0], amps, (1, 2), wk, z)

    def put(read):
        def sink(v, block):
            for (a, b), out in zip(CUTS, outs):
                if a <= v < b:
                    out[v - a] = read(v, block).astype(BF16)

        return sink

    def keep(v, block):
        acc[v] = block

    last_step(amps, (1, 2), z, keep)
    if site == 0:
        fetch.wait()

    @pl.when(count >= 2)
    def _():
        if site:
            form_left(prior, left, grouped(lefts))
        amps = {3: pick_amp(core, site, amp_refs, prior, 3)}
        first_steps(left, amps, (3,), wk, z)
        last_step(amps, (3,), z, put(lambda v, block: acc[v] + block))

    @pl.when(count < 2)
    def _():
        for (a, b), out in zip(CUTS, outs):
            out[...] = acc[a:b].astype(BF16)


def q_kernel(site, sizes, lefts, amp_refs, w_own, w_oth, outs, left, wk, z, next_one, next_two, *sems):
    out = outs[0]
    lefts, y_refs = lefts[:-N_CUT], lefts[-N_CUT:]
    count, core, owner = place(sizes)
    step = pl.program_id(0)

    def fetch(slot):
        return pltpu.make_async_copy(lefts[0].at[slot], left.at[slot % 2], sems[0].at[slot % 2])

    @pl.when(step == 0)
    def _():
        if site == 0:
            fetch(0).start()
        expand_operator(core, site, (0, 1, 2, 3), w_own, w_oth, wk)
        next_one[...] = jnp.zeros_like(next_one)
        next_two[...] = jnp.zeros_like(next_two)

    if site == 0:
        @pl.when(step + 1 < count)
        def _():
            fetch(step + 1).start()

        for s in range(4):
            later_amp = jnp.where(core == 1, amp_refs[0][step, s].astype(F32), amp_refs[1][step, s].astype(F32))
            outs[1][step, s] = later_amp.astype(BF16)

        @pl.when(step < count)
        def _():
            fetch(step).wait()

        source = left.at[step % 2]
    else:
        @pl.when(step < count)
        def _():
            form_left(step, left, grouped(lefts))

        source = left

    @pl.when(jnp.logical_and(step == 1, owner > 0))
    def _():
        for (a, b), ref in zip(CUTS, y_refs):
            next_one[a:b] = next_one[a:b] + ref[...].astype(F32)

    def sink_zero(v, block):
        out[step, v] = (block + next_one[v]).astype(BF16)

    def sink_one(v, block):
        next_one[v] = block + next_two[v]

    def sink_two(v, block):
        next_two[v] = block

    def work(states):
        amps = {s: pick_amp(core, site, amp_refs, step, s) for s in states}
        first_steps(source, amps, states, wk, z)
        last_step(amps, (0,), z, sink_zero)
        if 1 in states:
            last_step(amps, (1, 2), z, sink_one)
        if 3 in states:
            last_step(amps, (3,), z, sink_two)

    @pl.when(step < count - 2)
    def _():
        work((0, 3, 1, 2))

    @pl.when(jnp.logical_and(step == count - 2, step >= 0))
    def _():
        work((0, 1, 2))

    @pl.when(step == count - 1)
    def _():
        work((0,))

    @pl.when(step >= count)
    def _():
        out[step] = jnp.zeros((HALF, S, S), BF16)


CUT_SHAPES = [(b - a, S, S) for a, b in CUTS]


def call(kernel, site, grid, left_specs, shapes, scratch, flops, sizes, lefts, amps, ops, after=()):
    n_left, n_out, n_after, n_amp = len(lefts), len(shapes), len(after), len(amps)

    def body(sizes, *refs):
        left_refs, refs = refs[:n_left], refs[n_left:]
        amp_refs, op_refs, refs = refs[:n_amp], refs[n_amp : n_amp + 2], refs[n_amp + 2 + n_after :]
        kernel(site, sizes, left_refs, amp_refs, *op_refs, refs[:n_out], *refs[n_out:])

    return pl.pallas_call(
        body,
        grid_spec=pltpu.PrefetchScalarGridSpec(
            num_scalar_prefetch=1,
            grid=(grid,),
            in_specs=left_specs + [VMEM] * (n_amp + 2) + [ANY] * n_after,
            out_specs=[VMEM] * n_out,
            scratch_shapes=scratch,
        ),
        out_shape=[jax.ShapeDtypeStruct(shape, BF16) for shape in shapes],
        cost_estimate=pl.CostEstimate(flops=flops, bytes_accessed=4_000_000, transcendentals=0),
        compiler_params=pltpu.CompilerParams(vmem_limit_bytes=24 * MIB, dimension_semantics=("arbitrary",)),
        name=kernel.__name__ + str(site),
    )(sizes, *lefts, *amps, *ops, *after)


def work_space():
    return [pltpu.VMEM((3, 16 * HALF, 16 * W), BF16), pltpu.VMEM((4, HALF, S, S), BF16)]


def edge_two(site, sizes, lefts, amps, ops):
    left = pltpu.VMEM((W, S, S) if site else (1, 8, S), BF16)
    return call(
        y_kernel, site, 1, [VMEM] * len(lefts), CUT_SHAPES, [left] + work_space(), 2_000_000_000, sizes, lefts, amps, ops
    )


def edge_one(site, sizes, lefts, amps, ops, after):
    scratch = [pltpu.VMEM((W, S, S), BF16)] + work_space() + [pltpu.VMEM((HALF, S, S), F32)]
    specs = [VMEM] * len(lefts)
    if site == 0:
        scratch.append(pltpu.SemaphoreType.DMA)
        specs = [VMEM, HBM]
    return call(x_kernel, site, 1, specs, CUT_SHAPES, scratch, 4_000_000_000, sizes, lefts, amps, ops, after)


def inner(site, sizes, lefts, amps, ops, after):
    left = pltpu.VMEM((W, S, S) if site else (2, W, S, S), BF16)
    scratch = [left] + work_space() + [pltpu.VMEM((HALF, S, S), F32)] * 2
    specs, shapes = [VMEM] * len(lefts), [(4, HALF, S, S)]
    if site == 0:
        scratch.append(pltpu.SemaphoreType.DMA((2,)))
        specs, shapes = [HBM] + [VMEM] * N_CUT, shapes + [(4, 4, S, S)]
    return call(q_kernel, site, 4, specs, shapes, scratch, Q_FLOPS, sizes, lefts, amps, ops, after)


def fetch_last(sizes, env):
    def body(sizes, env, out, sem):
        copy = pltpu.make_async_copy(env.at[place(sizes)[0] - 1], out, sem)
        copy.start()
        copy.wait()

    return pl.pallas_call(
        body,
        in_specs=[pl.BlockSpec(memory_space=pltpu.SMEM), HBM],
        out_specs=VMEM,
        scratch_shapes=[pltpu.SemaphoreType.DMA],
        out_shape=jax.ShapeDtypeStruct((W, S, S), BF16),
        compiler_params=pltpu.CompilerParams(vmem_limit_bytes=52 * MIB),
        name="fetch_last",
    )(sizes, env)


def block_copies(site, slots, blocks, out, sems):
    copies = []

    def add(ref, slot, v, length):
        copies.append(pltpu.make_async_copy(ref, out.at[slot, v : v + length], sems.at[len(copies)]))

    for slot in slots:
        for half in range(2):
            which = half if site == 0 else 1 - half
            if slot == 0:
                for (a, b), ref in zip(CUTS, blocks[slot][which]):
                    add(ref, slot, half * HALF + a, b - a)
            else:
                add(blocks[slot][which], slot, half * HALF, HALF)
    for copy in copies:
        copy.start()
    for copy in copies:
        copy.wait()


def finish_early(sizes, first, second):
    n_first, n_in = len(first), len(first) + len(second)

    def body(sizes, *refs):
        one = grouped(refs[:n_first])
        two_refs = refs[n_first:n_in]
        two = (None, *((two_refs[k], two_refs[3 + k]) for k in range(3)))
        out, sems = refs[n_in:]
        core = lax.axis_index("site")

        @pl.when(core == 0)
        def _():
            block_copies(0, range(4), one, out, sems)

        @pl.when(core == 1)
        def _():
            block_copies(1, range(1, 4), two, out, sems)

    return pl.pallas_call(
        body,
        in_specs=[pl.BlockSpec(memory_space=pltpu.SMEM)] + [VMEM] * n_in,
        out_specs=HBM,
        scratch_shapes=[pltpu.SemaphoreType.DMA((2 * N_CUT + 6,))],
        out_shape=jax.ShapeDtypeStruct((4, W, S, S), BF16),
        cost_estimate=pl.CostEstimate(flops=1000, bytes_accessed=1000, transcendentals=0),
        compiler_params=pltpu.CompilerParams(vmem_limit_bytes=4 * MIB),
        name="finish_early",
    )(sizes, *first, *second)


def finish_late(written, own, other):
    def body(written, *refs):
        out, sems = refs[2 * N_CUT :]

        @pl.when(lax.axis_index("site") == 1)
        def _():
            block_copies(1, (0,), ((refs[:N_CUT], refs[N_CUT : 2 * N_CUT]),), out, sems)

    return pl.pallas_call(
        body,
        in_specs=[HBM] + [VMEM] * (2 * N_CUT),
        out_specs=HBM,
        scratch_shapes=[pltpu.SemaphoreType.DMA((2 * N_CUT,))],
        out_shape=jax.ShapeDtypeStruct((4, W, S, S), BF16),
        input_output_aliases={0: 0},
        compiler_params=pltpu.CompilerParams(vmem_limit_bytes=4 * MIB),
        name="finish_late",
    )(written, *own, *other)


def operator_blocks(weight, mask):
    kept = jnp.where(mask[:, None, None, :] != 0, weight, jnp.zeros_like(weight))
    return jnp.transpose(kept, (1, 2, 0, 3))


def later(x, *others):
    return lax.optimization_barrier((x, *others))[0]


def plus(x, y, take):
    return (x.astype(F32) + jnp.where(take, y.astype(F32), 0.0)).astype(BF16)


def shards(owners, environment, amplitudes, mpo_weight, mpo_mask, sector_count):
    owner = lax.axis_index("sector")
    across = [(c * owners + o, (1 - c) * owners + o) for c in range(2) for o in range(owners)]
    ahead = [(c * owners + o, c * owners + (o + 1) % owners) for c in range(2) for o in range(owners)]

    def swap(x):
        return lax.ppermute(x, AXES, across)

    def onward(x):
        return lax.ppermute(x, AXES, ahead)

    env = jnp.transpose(environment, (0, 2, 1, 3))
    own_ops = operator_blocks(mpo_weight[0], mpo_mask[0])
    amps = (amplitudes[0], swap(amplitudes[0]))
    ops = (own_ops, swap(own_ops))

    env_last = fetch_last(sector_count, env)
    edge_left, back_left, lefts = (env_last,), (env_last, env), (env,)
    inward = owner > 0
    for site in range(2):
        y_out = edge_two(site, sector_count, edge_left, amps, ops)
        y_in = [onward(y) for y in y_out]
        if site == 0:
            count = lax.dynamic_index_in_dim(later(sector_count, y_out[0]), owner, 0, keepdims=False)
            pass_on = jnp.logical_and(count == 1, inward)
        x_out = edge_one(site, sector_count, back_left, amps, ops, y_out)
        x_sent = [plus(x, y, pass_on) for x, y in zip(x_out, y_in)]
        x_in = [onward(x) for x in x_sent]
        made = inner(site, sector_count, (*lefts, *y_in), amps, ops, x_sent)
        inside = made[0]
        rest = [inside[k] for k in (1, 2, 3)]
        rest_oth = [swap(later(part, y_in[-1])) for part in rest]
        zero = [plus(later(inside, x)[0, a:b], x, inward) for (a, b), x in zip(CUTS, x_in)]
        if site == 0:
            zero_oth = [swap(block) for block in zero]
            lefts = edge_left = back_left = first = (*zero, *zero_oth, *rest, *rest_oth)
            amps = (made[1],)
        else:
            written = finish_early(sector_count, first, (*rest, *rest_oth))
            zero_oth = [swap(block) for block in zero]
            result = finish_late(written, zero, zero_oth)
    return jnp.transpose(result, (0, 2, 1, 3))[None]


def solution(mesh):
    placed = (
        P("sector", None, None, None),
        P("site", "sector", None, None, None),
        P("site", None, None, None, None),
        P("site", None, None),
        P(),
    )
    return jax.shard_map(
        functools.partial(shards, mesh.shape["sector"]),
        mesh=mesh,
        in_specs=placed,
        out_specs=P("site", "sector", None, None, None),
        check_vma=False,
    )
```

time: 829 us -> 81.2 us (0.10)
  the two profiles are of different devices: /device:TPU:70 before, /device:TPU:1 now
where the time goes in v1:
time: 81.2 us; the launch traced here: 81 us
  waiting for transfers between devices  42.2 us (52%)
  Pallas kernels  19.4 us (24%)
  starting transfers between devices  12.2 us (15%)
  local copies, waits for them, and re-layouts  3.69 us (5%)
  other arithmetic  2.34 us (3%)
  between operations  1.12 us (1%)
    ppermute x8, waiting for transfers between devices, onward(): return lax.ppermute(x, AXES, ahead)  40.7 us
    pallas_call x6, Pallas kernels, call(): pl.pallas_call(body, grid_spec=pltpu.PrefetchScalarGridSpec(num_scalar_pr...  14.4 us
    ppermute x12, starting transfers between devices, swap(): return lax.ppermute(x, AXES, across)  9.01 us
    ppermute x8, starting transfers between devices, onward(): return lax.ppermute(x, AXES, ahead)  3.19 us
    unnamed x11, local copies, waits for them, and re-layouts  2.78 us
    pallas_call x1, Pallas kernels, finish_early(): pl.pallas_call(body, in_specs=[pl.BlockSpec(memory_space=pltpu.SMEM)] + [...  2.25 us
    pallas_call x1, Pallas kernels, fetch_last(): pl.pallas_call(body, in_specs=[pl.BlockSpec(memory_space=pltpu.SMEM), HBM...  1.76 us
  transfers between devices with their start and end apart: 20, of which 8 were waited for; matrix products, arithmetic and copies ran while one was open for 4% of the time, Pallas kernels for 19%

profile of v1, /device:TPU:1, one launch (start us, length us, event | category | flops | bytes accessed | tf_op | source)
XLA Modules:
  0.0 81.0 jit_solution(14348900551572674241)
XLA Ops:
  0.0 1.4 %collective-permute-start = (bf16[4,4,128,128]{3,2,1,0:T(8,128)(2,1)}, bf16[4,4,128,128]{3,2,1,0:T(8,128)(2,1)S(1)}, u32[]{:S(2)}, u32[]{:S(2)}) collective-permute-start(bf16[4,4,128,128]{3,2,1,0:T(8,128)(2,1)} %bitcast.42), channel_id=1, source_target_pairs={{0,64},{1,65},{2,66},{3,67},{4,68},{5,69},{6,70},{7,71},{8,72},{9,... | collective-permute-start | bytes 1572872 | tf_op jit(solution)/shard_map/ppermute | solution.py:429
  3.9 1.8 %fetch_last.1.refs_0_ = bf16[30,128,128]{2,1,0:T(8,128)(2,1)S(1)} custom-call(s32[64]{0:T(128)S(1)} %copy-done.2, bf16[4,30,128,128]{3,2,1,0:T(8,128)(2,1)} %bitcast.39), custom_call_target="tpu_custom_call" | custom-call | tf_op jit(solution)/shard_map/fetch_last/pallas_call | solution.py:329
  5.7 1.5 %y_kernel0.1 = (bf16[8,128,128]{2,1,0:T(8,128)(2,1)S(1)}, bf16[7,128,128]{2,1,0:T(8,128)(2,1)S(1)}) custom-call(s32[64]{0:T(128)S(1)} %copy-done.2, bf16[30,128,128]{2,1,0:T(8,128)(2,1)S(1)} %fetch_last.1.refs_0_, bf16[4,4,128,128]{3,2,1,0:T(8,128)(2,1)S(1)} %bitcast.43, bf16[4,4,128,128]{3,2,1,0:T(8,128)(2,1)S(1)} %collective-permute-done.refs_2_.refs_3_.refs_4_, ...), custom_call_target="tpu_custom_call" | custom-call | flops 2000000000 | bytes 4000000 | tf_op jit(solution)/shard_map/y_kernel0/pallas_call | solution.py:277
  7.2 1.4 %collective-permute-start.3 = (bf16[7,128,128]{2,1,0:T(8,128)(2,1)S(1)}, bf16[7,128,128]{2,1,0:T(8,128)(2,1)S(1)}, u32[]{:S(2)}, u32[]{:S(2)}) collective-permute-start(bf16[7,128,128]{2,1,0:T(8,128)(2,1)S(1)} %get-tuple-element.27.refs_7_), channel_id=1, source_target_pairs={{0,1},{1,2},{2,3},{3,4},{4,5},{5,6},{6,7},{7,8},{8,9},{9,10},{10,1... | collective-permute-start | bytes 688136 | tf_op jit(solution)/shard_map/ppermute | solution.py:432
  8.6 1.3 %collective-permute-start.2 = (bf16[8,128,128]{2,1,0:T(8,128)(2,1)S(1)}, bf16[8,128,128]{2,1,0:T(8,128)(2,1)S(1)}, u32[]{:S(2)}, u32[]{:S(2)}) collective-permute-start(bf16[8,128,128]{2,1,0:T(8,128)(2,1)S(1)} %get-tuple-element.26.refs_6_), channel_id=1, source_target_pairs={{0,1},{1,2},{2,3},{3,4},{4,5},{5,6},{6,7},{7,8},{8,9},{9,10},{10,1... | collective-permute-start | bytes 786440 | tf_op jit(solution)/shard_map/ppermute | solution.py:432
  9.9 2.7 %x_kernel0.1 = (bf16[8,128,128]{2,1,0:T(8,128)(2,1)S(1)}, bf16[7,128,128]{2,1,0:T(8,128)(2,1)S(1)}) custom-call(s32[64]{0:T(128)S(1)} %copy-done.2, bf16[30,128,128]{2,1,0:T(8,128)(2,1)S(1)} %fetch_last.1.refs_0_, bf16[4,30,128,128]{3,2,1,0:T(8,128)(2,1)S(1)} %bitcast.40, bf16[4,4,128,128]{3,2,1,0:T(8,128)(2,1)S(1)} %bitcast.44, ...), custom_call_target="tpu_custom_call" | custom-call | flops 4000000000 | bytes 4000000 | tf_op jit(solution)/shard_map/x_kernel0/pallas_call | solution.py:277
  13.9 7.4 %collective-permute-done.3.refs_2_ = bf16[7,128,128]{2,1,0:T(8,128)(2,1)S(1)} collective-permute-done((bf16[7,128,128]{2,1,0:T(8,128)(2,1)S(1)}, bf16[7,128,128]{2,1,0:T(8,128)(2,1)S(1)}, u32[]{:S(2)}, u32[]{:S(2)}) %collective-permute-start.3) | collective-permute-done | bytes 229408 | tf_op jit(solution)/shard_map/ppermute | solution.py:432
  21.5 5.5 %collective-permute-done.2.refs_1_ = bf16[8,128,128]{2,1,0:T(8,128)(2,1)S(1)} collective-permute-done((bf16[8,128,128]{2,1,0:T(8,128)(2,1)S(1)}, bf16[8,128,128]{2,1,0:T(8,128)(2,1)S(1)}, u32[]{:S(2)}, u32[]{:S(2)}) %collective-permute-start.2) | collective-permute-done | bytes 262176 | tf_op jit(solution)/shard_map/ppermute | solution.py:432
  27.1 2.1 %copy-done.1 = bf16[4,128,30,128]{3,1,2,0:T(8,128)(2,1)S(1)} copy-done((bf16[4,128,30,128]{3,1,2,0:T(8,128)(2,1)S(1)}, bf16[4,128,30,128]{3,1,2,0:T(8,128)(2,1)}, u32[]{:S(2)}) %copy-start.1) | copy-done | bytes 3932184
  29.2 3.1 %q_kernel0.1 = (bf16[4,15,128,128]{3,2,1,0:T(8,128)(2,1)S(1)}, bf16[4,4,128,128]{3,2,1,0:T(8,128)(2,1)S(1)}) custom-call(s32[64]{0:T(128)S(1)} %copy-done.3, bf16[4,30,128,128]{3,2,1,0:T(8,128)(2,1)S(1)} %bitcast.41, bf16[8,128,128]{2,1,0:T(8,128)(2,1)S(1)} %collective-permute-done.2.refs_1_, bf16[7,128,128]{2,1,0:T(8,128)(2,1)S(1)} %collective-permute-done.3.refs_2_, ...), custom_call_target="tpu_custom_call" | custom-call | flops 8000000000 | bytes 4000000 | tf_op jit(solution)/shard_map/q_kernel0/pallas_call | solution.py:277
  32.5 1.1 %collective-permute-start.8 = (bf16[15,128,128]{2,1,0:T(8,128)(2,1)S(1)}, bf16[15,128,128]{2,1,0:T(8,128)(2,1)S(1)}, u32[]{:S(2)}, u32[]{:S(2)}) collective-permute-start(bf16[15,128,128]{2,1,0:T(8,128)(2,1)S(1)} %get-tuple-element.34.refs_4_), channel_id=1, source_target_pairs={{0,64},{1,65},{2,66},{3,67},{4,68},{5,69},{6,70},{7,71},{8,72},{9,... | collective-permute-start | bytes 1474568 | tf_op jit(solution)/shard_map/ppermute | solution.py:429
  34.1 5.2 %collective-permute-done.4 = bf16[8,128,128]{2,1,0:T(8,128)(2,1)S(1)} collective-permute-done((bf16[8,128,128]{2,1,0:T(8,128)(2,1)S(1)}, bf16[8,128,128]{2,1,0:T(8,128)(2,1)S(1)}, u32[]{:S(2)}, u32[]{:S(2)}) %collective-permute-start.4) | collective-permute-done | bytes 262176 | tf_op jit(solution)/shard_map/ppermute | solution.py:432
  39.4 2.0 %collective-permute-start.6 = (bf16[8,128,128]{2,1,0:T(8,128)(2,1)S(1)}, bf16[8,128,128]{2,1,0:T(8,128)(2,1)S(1)}, u32[]{:S(2)}, u32[]{:S(2)}) collective-permute-start(bf16[8,128,128]{2,1,0:T(8,128)(2,1)S(1)} %fusion.1.refs_0_), channel_id=1, source_target_pairs={{0,64},{1,65},{2,66},{3,67},{4,68},{5,69},{6,70},{7,71},{8,72},{9,... | collective-permute-start | bytes 786440 | tf_op jit(solution)/shard_map/ppermute | solution.py:429
  41.6 1.5 %collective-permute-done.7.refs_3_ = bf16[7,128,128]{2,1,0:T(8,128)(2,1)S(1)} collective-permute-done((bf16[7,128,128]{2,1,0:T(8,128)(2,1)S(1)}, bf16[7,128,128]{2,1,0:T(8,128)(2,1)S(1)}, u32[]{:S(2)}, u32[]{:S(2)}) %collective-permute-start.7) | collective-permute-done | bytes 229408 | tf_op jit(solution)/shard_map/ppermute | solution.py:429
  43.1 1.7 %y_kernel1.1 = (bf16[8,128,128]{2,1,0:T(8,128)(2,1)S(1)}, bf16[7,128,128]{2,1,0:T(8,128)(2,1)S(1)}) custom-call(s32[64]{0:T(128)S(1)} %copy-done.3, bf16[8,128,128]{2,1,0:T(8,128)(2,1)S(1)} %fusion.1.refs_0_, bf16[7,128,128]{2,1,0:T(8,128)(2,1)S(1)} %fusion.3.refs_1_, bf16[8,128,128]{2,1,0:T(8,128)(2,1)S(1)} %collective-permute-done.6.refs_2_, ...), custom_call_target="tpu_custom_call" | custom-call | flops 2000000000 | bytes 4000000 | tf_op jit(solution)/shard_map/y_kernel1/pallas_call | solution.py:277
  44.9 2.7 %x_kernel1.1 = (bf16[8,128,128]{2,1,0:T(8,128)(2,1)S(1)}, bf16[7,128,128]{2,1,0:T(8,128)(2,1)S(1)}) custom-call(s32[64]{0:T(128)S(1)} %copy-done.3, bf16[8,128,128]{2,1,0:T(8,128)(2,1)S(1)} %fusion.1.refs_0_, bf16[7,128,128]{2,1,0:T(8,128)(2,1)S(1)} %fusion.3.refs_1_, bf16[8,128,128]{2,1,0:T(8,128)(2,1)S(1)} %collective-permute-done.6.refs_2_, ...), custom_call_target="tpu_custom_call" | custom-call | flops 4000000000 | bytes 4000000 | tf_op jit(solution)/shard_map/x_kernel1/pallas_call | solution.py:277
  47.6 9.6 %collective-permute-done.12.refs_11_ = bf16[7,128,128]{2,1,0:T(8,128)(2,1)S(1)} collective-permute-done((bf16[7,128,128]{2,1,0:T(8,128)(2,1)S(1)}, bf16[7,128,128]{2,1,0:T(8,128)(2,1)S(1)}, u32[]{:S(2)}, u32[]{:S(2)}) %collective-permute-start.12) | collective-permute-done | bytes 229408 | tf_op jit(solution)/shard_map/ppermute | solution.py:432
  57.4 5.5 %collective-permute-done.11.refs_10_ = bf16[8,128,128]{2,1,0:T(8,128)(2,1)S(1)} collective-permute-done((bf16[8,128,128]{2,1,0:T(8,128)(2,1)S(1)}, bf16[8,128,128]{2,1,0:T(8,128)(2,1)S(1)}, u32[]{:S(2)}, u32[]{:S(2)}) %collective-permute-start.11) | collective-permute-done | bytes 262176 | tf_op jit(solution)/shard_map/ppermute | solution.py:432
  63.0 2.7 %q_kernel1.1 = bf16[4,15,128,128]{3,2,1,0:T(8,128)(2,1)S(1)} custom-call(s32[64]{0:T(128)S(1)} %copy-done.3, bf16[8,128,128]{2,1,0:T(8,128)(2,1)S(1)} %fusion.1.refs_0_, bf16[7,128,128]{2,1,0:T(8,128)(2,1)S(1)} %fusion.3.refs_1_, bf16[8,128,128]{2,1,0:T(8,128)(2,1)S(1)} %collective-permute-done.6.refs_2_, ...), custom_call_target="tpu_custom_call" | custom-call | flops 8000000000 | bytes 4000000 | tf_op jit(solution)/shard_map/q_kernel1/pallas_call | solution.py:277
  65.9 1.1 %collective-permute-start.13 = (bf16[15,128,128]{2,1,0:T(8,128)(2,1)S(1)}, bf16[15,128,128]{2,1,0:T(8,128)(2,1)S(1)}, u32[]{:S(2)}, u32[]{:S(2)}) collective-permute-start(bf16[15,128,128]{2,1,0:T(8,128)(2,1)S(1)} %get-tuple-element.42.refs_10_), channel_id=1, source_target_pairs={{0,64},{1,65},{2,66},{3,67},{4,68},{5,69},{6,70},{7,71},{8,72},{9,... | collective-permute-start | bytes 1474568 | tf_op jit(solution)/shard_map/ppermute | solution.py:429
  68.2 7.0 %collective-permute-done.16 = bf16[8,128,128]{2,1,0:T(8,128)(2,1)S(1)} collective-permute-done((bf16[8,128,128]{2,1,0:T(8,128)(2,1)S(1)}, bf16[8,128,128]{2,1,0:T(8,128)(2,1)S(1)}, u32[]{:S(2)}, u32[]{:S(2)}) %collective-permute-start.16) | collective-permute-done | bytes 262176 | tf_op jit(solution)/shard_map/ppermute | solution.py:432
  75.3 2.0 %collective-permute-start.18 = (bf16[8,128,128]{2,1,0:T(8,128)(2,1)S(1)}, bf16[8,128,128]{2,1,0:T(8,128)(2,1)S(1)}, u32[]{:S(2)}, u32[]{:S(2)}) collective-permute-start(bf16[8,128,128]{2,1,0:T(8,128)(2,1)S(1)} %fusion.refs_0_), channel_id=1, source_target_pairs={{0,64},{1,65},{2,66},{3,67},{4,68},{5,69},{6,70},{7,71},{8,72},{9,... | collective-permute-start | bytes 786440 | tf_op jit(solution)/shard_map/ppermute | solution.py:429
  77.5 2.3 %finish_early.1.written = bf16[4,30,128,128]{3,2,1,0:T(8,128)(2,1)} custom-call(s32[64]{0:T(128)S(1)} %copy-done.3, bf16[8,128,128]{2,1,0:T(8,128)(2,1)S(1)} %fusion.1.refs_0_, bf16[7,128,128]{2,1,0:T(8,128)(2,1)S(1)} %fusion.3.refs_1_, bf16[8,128,128]{2,1,0:T(8,128)(2,1)S(1)} %collective-permute-done.6.refs_2_, ...), custom_call_target="tpu_custom_call" | custom-call | flops 1000 | bytes 1000 | tf_op jit(solution)/shard_map/finish_early/pallas_call | solution.py:378
  79.8 1.0 %finish_late.1 = bf16[4,30,128,128]{3,2,1,0:T(8,128)(2,1)} custom-call(bf16[4,30,128,128]{3,2,1,0:T(8,128)(2,1)} %finish_early.1.written, bf16[8,128,128]{2,1,0:T(8,128)(2,1)S(1)} %fusion.refs_0_, bf16[7,128,128]{2,1,0:T(8,128)(2,1)S(1)} %fusion.2.refs_1_, bf16[8,128,128]{2,1,0:T(8,128)(2,1)S(1)} %collective-permute-done.18.refs_2_, ...), custom_call_target="tpu_custom_call", output_to_operand_aliasing={{}: (0, {})} | custom-call | tf_op jit(solution)/shard_map/finish_late/pallas_call | solution.py:398
  (49 shorter events, 6.4 us)
Async XLA Ops:
  0.0 5.7 %collective-permute-start = (bf16[4,4,128,128]{3,2,1,0:T(8,128)(2,1)}, bf16[4,4,128,128]{3,2,1,0:T(8,128)(2,1)S(1)}, u32[]{:S(2)}, u32[]{:S(2)}) collective-permute-start(bf16[4,4,128,128]{3,2,1,0:T(8,128)(2,1)} %bitcast.42), channel_id=1, source_target_pairs={{0,64},{1,65},{2,66},{3,67},{4,68},{5,69},{6,70},{7,71},{8,72},{9,... | collective-permute-start | bytes 1572872 | tf_op jit(solution)/shard_map/ppermute | solution.py:429
  3.1 2.5 %collective-permute-start.1 = (bf16[4,4,30,30]{3,2,1,0:T(8,128)(2,1)S(1)}, bf16[4,4,30,30]{3,2,1,0:T(8,128)(2,1)S(1)}, u32[]{:S(2)}, u32[]{:S(2)}) collective-permute-start(bf16[4,4,30,30]{3,2,1,0:T(8,128)(2,1)S(1)} %fusion.4.refs_3_.refs_4_.refs_5_.refs_11_.refs_13_), channel_id=1, source_target_pairs={{0,64},{1,65},{2,66},{3,67},{4,68},{5,69},{6,70},{7,71},{8,72},{9,... | collective-permute-start | bytes 86408 | tf_op jit(solution)/shard_map/ppermute | solution.py:429
  3.9 1.8 %copy-start.4 = (bf16[1,4,4,128,128]{4,3,2,1,0:T(8,128)(2,1)S(1)}, bf16[1,4,4,128,128]{4,3,2,1,0:T(8,128)(2,1)}, u32[]{:S(2)}) copy-start(bf16[1,4,4,128,128]{4,3,2,1,0:T(8,128)(2,1)} %param.6) | copy-start | bytes 1572868
  5.6 4.3 %copy-start = (bf16[4,128,30,128]{3,1,2,0:T(8,128)(2,1)S(1)}, bf16[4,128,30,128]{3,1,2,0:T(8,128)(2,1)}, u32[]{:S(2)}) copy-start(bf16[4,128,30,128]{3,1,2,0:T(8,128)(2,1)} %param.5) | copy-start | bytes 11796484
  7.2 14.1 %collective-permute-start.3 = (bf16[7,128,128]{2,1,0:T(8,128)(2,1)S(1)}, bf16[7,128,128]{2,1,0:T(8,128)(2,1)S(1)}, u32[]{:S(2)}, u32[]{:S(2)}) collective-permute-start(bf16[7,128,128]{2,1,0:T(8,128)(2,1)S(1)} %get-tuple-element.27.refs_7_), channel_id=1, source_target_pairs={{0,1},{1,2},{2,3},{3,4},{4,5},{5,6},{6,7},{7,8},{8,9},{9,10},{10,1... | collective-permute-start | bytes 688136 | tf_op jit(solution)/shard_map/ppermute | solution.py:432
  8.6 18.4 %copy-start.3 = (s32[64]{0:T(128)S(1)}, s32[64]{0:T(128)}, u32[]{:S(2)}) copy-start(s32[64]{0:T(128)} %sizes.15) | copy-start | bytes 772
  8.6 18.3 %collective-permute-start.2 = (bf16[8,128,128]{2,1,0:T(8,128)(2,1)S(1)}, bf16[8,128,128]{2,1,0:T(8,128)(2,1)S(1)}, u32[]{:S(2)}, u32[]{:S(2)}) collective-permute-start(bf16[8,128,128]{2,1,0:T(8,128)(2,1)S(1)} %get-tuple-element.26.refs_6_), channel_id=1, source_target_pairs={{0,1},{1,2},{2,3},{3,4},{4,5},{5,6},{6,7},{7,8},{8,9},{9,10},{10,1... | collective-permute-start | bytes 786440 | tf_op jit(solution)/shard_map/ppermute | solution.py:432
  21.4 12.7 %collective-permute-start.5 = (bf16[7,128,128]{2,1,0:T(8,128)(2,1)S(1)}, bf16[7,128,128]{2,1,0:T(8,128)(2,1)S(1)}, u32[]{:S(2)}, u32[]{:S(2)}) collective-permute-start(bf16[7,128,128]{2,1,0:T(8,128)(2,1)S(1)} %add_convert_fusion.3.refs_8_), channel_id=1, source_target_pairs={{0,1},{1,2},{2,3},{3,4},{4,5},{5,6},{6,7},{7,8},{8,9},{9,10},{10,1... | collective-permute-start | bytes 688136 | tf_op jit(solution)/shard_map/ppermute | solution.py:432
  27.0 12.3 %collective-permute-start.4 = (bf16[8,128,128]{2,1,0:T(8,128)(2,1)S(1)}, bf16[8,128,128]{2,1,0:T(8,128)(2,1)S(1)}, u32[]{:S(2)}, u32[]{:S(2)}) collective-permute-start(bf16[8,128,128]{2,1,0:T(8,128)(2,1)S(1)} %add_convert_fusion.1.refs_7_), channel_id=1, source_target_pairs={{0,1},{1,2},{2,3},{3,4},{4,5},{5,6},{6,7},{7,8},{8,9},{9,10},{10,1... | collective-permute-start | bytes 786440 | tf_op jit(solution)/shard_map/ppermute | solution.py:432
  27.1 2.1 %copy-start.1 = (bf16[4,128,30,128]{3,1,2,0:T(8,128)(2,1)S(1)}, bf16[4,128,30,128]{3,1,2,0:T(8,128)(2,1)}, u32[]{:S(2)}) copy-start(bf16[4,128,30,128]{3,1,2,0:T(8,128)(2,1)} %param.5) | copy-start | bytes 11796484
  32.5 10.6 %collective-permute-start.8 = (bf16[15,128,128]{2,1,0:T(8,128)(2,1)S(1)}, bf16[15,128,128]{2,1,0:T(8,128)(2,1)S(1)}, u32[]{:S(2)}, u32[]{:S(2)}) collective-permute-start(bf16[15,128,128]{2,1,0:T(8,128)(2,1)S(1)} %get-tuple-element.34.refs_4_), channel_id=1, source_target_pairs={{0,64},{1,65},{2,66},{3,67},{4,68},{5,69},{6,70},{7,71},{8,72},{9,... | collective-permute-start | bytes 1474568 | tf_op jit(solution)/shard_map/ppermute | solution.py:429
  33.6 9.5 %collective-permute-start.9 = (bf16[15,128,128]{2,1,0:T(8,128)(2,1)S(1)}, bf16[15,128,128]{2,1,0:T(8,128)(2,1)S(1)}, u32[]{:S(2)}, u32[]{:S(2)}) collective-permute-start(bf16[15,128,128]{2,1,0:T(8,128)(2,1)S(1)} %get-tuple-element.35.refs_5_), channel_id=1, source_target_pairs={{0,64},{1,65},{2,66},{3,67},{4,68},{5,69},{6,70},{7,71},{8,72},{9,... | collective-permute-start | bytes 1474568 | tf_op jit(solution)/shard_map/ppermute | solution.py:429
  33.7 9.4 %collective-permute-start.10 = (bf16[15,128,128]{2,1,0:T(8,128)(2,1)S(1)}, bf16[15,128,128]{2,1,0:T(8,128)(2,1)S(1)}, u32[]{:S(2)}, u32[]{:S(2)}) collective-permute-start(bf16[15,128,128]{2,1,0:T(8,128)(2,1)S(1)} %get-tuple-element.36.refs_6_), channel_id=1, source_target_pairs={{0,64},{1,65},{2,66},{3,67},{4,68},{5,69},{6,70},{7,71},{8,72},{9,... | collective-permute-start | bytes 1474568 | tf_op jit(solution)/shard_map/ppermute | solution.py:429
  39.4 3.7 %collective-permute-start.6 = (bf16[8,128,128]{2,1,0:T(8,128)(2,1)S(1)}, bf16[8,128,128]{2,1,0:T(8,128)(2,1)S(1)}, u32[]{:S(2)}, u32[]{:S(2)}) collective-permute-start(bf16[8,128,128]{2,1,0:T(8,128)(2,1)S(1)} %fusion.1.refs_0_), channel_id=1, source_target_pairs={{0,64},{1,65},{2,66},{3,67},{4,68},{5,69},{6,70},{7,71},{8,72},{9,... | collective-permute-start | bytes 786440 | tf_op jit(solution)/shard_map/ppermute | solution.py:429
  41.5 1.6 %collective-permute-start.7 = (bf16[7,128,128]{2,1,0:T(8,128)(2,1)S(1)}, bf16[7,128,128]{2,1,0:T(8,128)(2,1)S(1)}, u32[]{:S(2)}, u32[]{:S(2)}) collective-permute-start(bf16[7,128,128]{2,1,0:T(8,128)(2,1)S(1)} %fusion.3.refs_1_), channel_id=1, source_target_pairs={{0,64},{1,65},{2,66},{3,67},{4,68},{5,69},{6,70},{7,71},{8,72},{9,... | collective-permute-start | bytes 688136 | tf_op jit(solution)/shard_map/ppermute | solution.py:429
  44.7 12.5 %collective-permute-start.12 = (bf16[7,128,128]{2,1,0:T(8,128)(2,1)S(1)}, bf16[7,128,128]{2,1,0:T(8,128)(2,1)S(1)}, u32[]{:S(2)}, u32[]{:S(2)}) collective-permute-start(bf16[7,128,128]{2,1,0:T(8,128)(2,1)S(1)} %get-tuple-element.39.refs_14_), channel_id=1, source_target_pairs={{0,1},{1,2},{2,3},{3,4},{4,5},{5,6},{6,7},{7,8},{8,9},{9,10},{10,1... | collective-permute-start | bytes 688136 | tf_op jit(solution)/shard_map/ppermute | solution.py:432
  44.8 18.0 %collective-permute-start.11 = (bf16[8,128,128]{2,1,0:T(8,128)(2,1)S(1)}, bf16[8,128,128]{2,1,0:T(8,128)(2,1)S(1)}, u32[]{:S(2)}, u32[]{:S(2)}) collective-permute-start(bf16[8,128,128]{2,1,0:T(8,128)(2,1)S(1)} %get-tuple-element.38.refs_13_), channel_id=1, source_target_pairs={{0,1},{1,2},{2,3},{3,4},{4,5},{5,6},{6,7},{7,8},{8,9},{9,10},{10,1... | collective-permute-start | bytes 786440 | tf_op jit(solution)/shard_map/ppermute | solution.py:432
  57.3 10.9 %collective-permute-start.17 = (bf16[7,128,128]{2,1,0:T(8,128)(2,1)S(1)}, bf16[7,128,128]{2,1,0:T(8,128)(2,1)S(1)}, u32[]{:S(2)}, u32[]{:S(2)}) collective-permute-start(bf16[7,128,128]{2,1,0:T(8,128)(2,1)S(1)} %add_convert_fusion.2.refs_16_), channel_id=1, source_target_pairs={{0,1},{1,2},{2,3},{3,4},{4,5},{5,6},{6,7},{7,8},{8,9},{9,10},{10,1... | collective-permute-start | bytes 688136 | tf_op jit(solution)/shard_map/ppermute | solution.py:432
  62.9 12.3 %collective-permute-start.16 = (bf16[8,128,128]{2,1,0:T(8,128)(2,1)S(1)}, bf16[8,128,128]{2,1,0:T(8,128)(2,1)S(1)}, u32[]{:S(2)}, u32[]{:S(2)}) collective-permute-start(bf16[8,128,128]{2,1,0:T(8,128)(2,1)S(1)} %add_convert_fusion.refs_15_), channel_id=1, source_target_pairs={{0,1},{1,2},{2,3},{3,4},{4,5},{5,6},{6,7},{7,8},{8,9},{9,10},{10,1... | collective-permute-start | bytes 786440 | tf_op jit(solution)/shard_map/ppermute | solution.py:432
  65.9 11.6 %collective-permute-start.13 = (bf16[15,128,128]{2,1,0:T(8,128)(2,1)S(1)}, bf16[15,128,128]{2,1,0:T(8,128)(2,1)S(1)}, u32[]{:S(2)}, u32[]{:S(2)}) collective-permute-start(bf16[15,128,128]{2,1,0:T(8,128)(2,1)S(1)} %get-tuple-element.42.refs_10_), channel_id=1, source_target_pairs={{0,64},{1,65},{2,66},{3,67},{4,68},{5,69},{6,70},{7,71},{8,72},{9,... | collective-permute-start | bytes 1474568 | tf_op jit(solution)/shard_map/ppermute | solution.py:429
  67.0 10.5 %collective-permute-start.14 = (bf16[15,128,128]{2,1,0:T(8,128)(2,1)S(1)}, bf16[15,128,128]{2,1,0:T(8,128)(2,1)S(1)}, u32[]{:S(2)}, u32[]{:S(2)}) collective-permute-start(bf16[15,128,128]{2,1,0:T(8,128)(2,1)S(1)} %get-tuple-element.43.refs_11_), channel_id=1, source_target_pairs={{0,64},{1,65},{2,66},{3,67},{4,68},{5,69},{6,70},{7,71},{8,72},{9,... | collective-permute-start | bytes 1474568 | tf_op jit(solution)/shard_map/ppermute | solution.py:429
  67.1 10.4 %collective-permute-start.15 = (bf16[15,128,128]{2,1,0:T(8,128)(2,1)S(1)}, bf16[15,128,128]{2,1,0:T(8,128)(2,1)S(1)}, u32[]{:S(2)}, u32[]{:S(2)}) collective-permute-start(bf16[15,128,128]{2,1,0:T(8,128)(2,1)S(1)} %get-tuple-element.44.refs_12_), channel_id=1, source_target_pairs={{0,64},{1,65},{2,66},{3,67},{4,68},{5,69},{6,70},{7,71},{8,72},{9,... | collective-permute-start | bytes 1474568 | tf_op jit(solution)/shard_map/ppermute | solution.py:429
  75.3 4.5 %collective-permute-start.18 = (bf16[8,128,128]{2,1,0:T(8,128)(2,1)S(1)}, bf16[8,128,128]{2,1,0:T(8,128)(2,1)S(1)}, u32[]{:S(2)}, u32[]{:S(2)}) collective-permute-start(bf16[8,128,128]{2,1,0:T(8,128)(2,1)S(1)} %fusion.refs_0_), channel_id=1, source_target_pairs={{0,64},{1,65},{2,66},{3,67},{4,68},{5,69},{6,70},{7,71},{8,72},{9,... | collective-permute-start | bytes 786440 | tf_op jit(solution)/shard_map/ppermute | solution.py:429
  77.4 2.4 %collective-permute-start.19 = (bf16[7,128,128]{2,1,0:T(8,128)(2,1)S(1)}, bf16[7,128,128]{2,1,0:T(8,128)(2,1)S(1)}, u32[]{:S(2)}, u32[]{:S(2)}) collective-permute-start(bf16[7,128,128]{2,1,0:T(8,128)(2,1)S(1)} %fusion.2.refs_1_), channel_id=1, source_target_pairs={{0,64},{1,65},{2,66},{3,67},{4,68},{5,69},{6,70},{7,71},{8,72},{9,... | collective-permute-start | bytes 688136 | tf_op jit(solution)/shard_map/ppermute | solution.py:429
  (1 other events, 0.7 us)
